TPU v7x, 128 devices: a whole 4x4x4 slice. The times are simulated.
128 devices in a mesh: group: 2 (over z_lo), seq: 8 (over x, core), head: 8 (over z_hi, y).
Axes of the slice: x: 4, y: 4, z: 4 (z_hi: 2, z_lo: 2; z = z_hi * 2 + z_lo), core: 2. Of those that a mesh axis runs over, the one named last changes fastest.
Arguments:
- prompt_kv: bfloat16 [2, 32768, 1024], P(None, ('group', 'seq'), 'head'), may hold values from -16 to 16
- queries: bfloat16 [3, 256, 16384], P(None, 'group', 'head'), may hold values from -32 to 32
- new_kv: bfloat16 [2, 3, 256, 1024], P(None, None, 'group', 'head'), may hold values from -16 to 16
- resident_kv: bfloat16 [2, 256, 1024, 1024], P(None, 'group', 'seq', 'head'), may hold values from -8 to 8
- seq_lengths: int32 [256], P('group'), may hold values from 1 to 1024, 131072 in all
Outputs:
- attended: bfloat16 [3, 256, 16384], P(None, 'group', 'head')
Inputs may be any that keep to these rules, and one draw needn't show every extreme that they name: `seq_lengths`: some sample has all 1024 slots valid.
All inputs are finite; a program needn't handle non-finite values. No bound on the sum of `seq_lengths` on one device may be relied on, other than what follows from the above.
Results may differ from a plain program's by a relative error of at most 0.0045.
Values may be sent and summed in bfloat16 or wider, within the bound.
A program may use at most 128 MiB of HBM per device.

v0:
```python
import math

import jax
import jax.numpy as jnp
from jax import lax
from jax.sharding import PartitionSpec as P

DH = 128


MASKED_SCORE = -1e30


def arrange_heads(rows_query, kv_dev):
    step_count, row_count, column_count = rows_query.shape
    group_size = column_count // (kv_dev * DH)
    shaped = rows_query.reshape(step_count, row_count, kv_dev, group_size, DH)
    return jnp.transpose(shaped, (2, 0, 1, 3, 4))


def empty_partial(query_heads):
    running_max = jnp.full(query_heads.shape[:-1], MASKED_SCORE, jnp.float32)
    running_sum = jnp.zeros(query_heads.shape[:-1], jnp.float32)
    running_out = jnp.zeros(query_heads.shape, jnp.float32)
    return (running_max, running_sum, running_out)


def absorb(partial_value, scores, mix_values):
    running_max, running_sum, running_out = partial_value
    new_max = jnp.maximum(running_max, jnp.max(scores, axis=-1))
    rescale = jnp.exp(running_max - new_max)
    weights = jnp.exp(scores - new_max[..., None])
    running_sum = running_sum * rescale + jnp.sum(weights, axis=-1)
    running_out = running_out * rescale[..., None] + mix_values(weights.astype(jnp.bfloat16))
    return (new_max, running_sum, running_out)


def prompt_pass(query_heads, partial_value, block_rows, logit_scale_factor):
    kv_dev = query_heads.shape[0]
    row_count = block_rows.shape[1]
    block_size = math.gcd(row_count, 512)

    def one_block(block_index, carry):
        sliced = lax.dynamic_slice_in_dim(block_rows, block_index * block_size, block_size, 1)
        key_block = sliced[0].reshape(block_size, kv_dev, DH)
        value_block = sliced[1].reshape(block_size, kv_dev, DH)
        scores = (
            jnp.einsum(
                "hsiad,nhd->hsian", query_heads, key_block, preferred_element_type=jnp.float32
            )
            * logit_scale_factor
        )

        def mix_values(weights):
            return jnp.einsum(
                "hsian,nhd->hsiad", weights, value_block, preferred_element_type=jnp.float32
            )

        return absorb(carry, scores, mix_values)

    return lax.fori_loop(0, row_count // block_size, one_block, partial_value)


def resident_pass(query_heads, partial_value, resident_kv, seq_lengths, offset, logit_scale_factor):
    kv_dev = query_heads.shape[0]
    row_count = resident_kv.shape[1]
    span_len = resident_kv.shape[2]
    key_block = resident_kv[0].reshape(row_count, span_len, kv_dev, DH)
    value_block = resident_kv[1].reshape(row_count, span_len, kv_dev, DH)
    scores = (
        jnp.einsum("hsiad,inhd->hsian", query_heads, key_block, preferred_element_type=jnp.float32)
        * logit_scale_factor
    )
    position = offset + jnp.arange(span_len, dtype=jnp.int32)
    visible = position[None, :] < seq_lengths[:, None]
    scores = jnp.where(visible[None, None, :, None, :], scores, MASKED_SCORE)

    def mix_values(weights):
        return jnp.einsum(
            "hsian,inhd->hsiad", weights, value_block, preferred_element_type=jnp.float32
        )

    return absorb(partial_value, scores, mix_values)


def new_pass(query_heads, partial_value, new_kv, logit_scale_factor):
    kv_dev = query_heads.shape[0]
    step_count = new_kv.shape[1]
    row_count = new_kv.shape[2]
    key_block = new_kv[0].reshape(step_count, row_count, kv_dev, DH)
    value_block = new_kv[1].reshape(step_count, row_count, kv_dev, DH)
    scores = (
        jnp.einsum("hsiad,tihd->hsiat", query_heads, key_block, preferred_element_type=jnp.float32)
        * logit_scale_factor
    )
    causal = (
        jnp.arange(step_count, dtype=jnp.int32)[None, :]
        <= jnp.arange(step_count, dtype=jnp.int32)[:, None]
    )
    scores = jnp.where(causal[None, :, None, None, :], scores, MASKED_SCORE)

    def mix_values(weights):
        return jnp.einsum(
            "hsiat,tihd->hsiad", weights, value_block, preferred_element_type=jnp.float32
        )

    return absorb(partial_value, scores, mix_values)


def local(prompt_kv, queries, new_kv, resident_kv, seq_lengths):
    logit_scale_factor = DH ** (-0.5)
    kv_dev = prompt_kv.shape[2] // DH
    own_rows = queries.shape[1]
    offset = lax.axis_index("seq") * resident_kv.shape[2]
    everyone = lax.all_gather(queries, "group", axis=1, tiled=True)
    query_heads = arrange_heads(everyone, kv_dev)
    partial_value = prompt_pass(
        query_heads, empty_partial(query_heads), prompt_kv, logit_scale_factor
    )
    row_start = lax.axis_index("group") * own_rows
    own_part = tuple(
        (lax.dynamic_slice_in_dim(sliced, row_start, own_rows, 2) for sliced in partial_value)
    )
    own_heads = lax.dynamic_slice_in_dim(query_heads, row_start, own_rows, 2)
    own_part = resident_pass(
        own_heads, own_part, resident_kv, seq_lengths, offset, logit_scale_factor
    )
    partial_value = tuple(
        (
            lax.dynamic_update_slice_in_dim(sliced, updated, row_start, 2)
            for sliced, updated in zip(partial_value, own_part)
        )
    )
    local_max, local_sum, local_out = partial_value
    global_max = lax.pmax(local_max, ("group", "seq"))
    rate = jnp.exp(local_max - global_max)
    shares = (
        lax.psum_scatter(local_sum * rate, "group", scatter_dimension=2, tiled=True),
        lax.psum_scatter(local_out * rate[..., None], "group", scatter_dimension=2, tiled=True),
    )
    summed = lax.psum((shares[0], shares[1]), "seq")
    own_max = lax.dynamic_slice_in_dim(global_max, row_start, own_rows, 2)
    partial_value = (own_max, summed[0], summed[1])
    query_heads = own_heads
    partial_value = new_pass(query_heads, partial_value, new_kv, logit_scale_factor)
    result = partial_value[2] / partial_value[1][..., None]
    result = jnp.transpose(result, (1, 2, 0, 3, 4)).reshape(queries.shape)
    return result.astype(jnp.bfloat16)


def solution(mesh):
    placed = (
        P(None, ("group", "seq"), "head"),
        P(None, "group", "head"),
        P(None, None, "group", "head"),
        P(None, "group", "seq", "head"),
        P("group"),
    )
    return jax.shard_map(
        local, mesh=mesh, in_specs=placed, out_specs=P(None, "group", "head"), check_vma=False
    )
```

profile of v0, /device:TPU:1, one launch (start us, length us, event | category | flops | bytes accessed | tf_op | source)
XLA Modules:
  0.0 471.8 jit_solution(376166352953849258)
XLA Ops:
  6.5 0.0 all-gather.2.cloned.1.call-start
  6.5 2.6 copy.50
  9.1 0.0 all-gather.2.cloned.1.call-update
  9.1 0.0 reduce-scatter.2.cloned.1.call-start
  9.2 0.0 copy-done.9
  9.3 0.1 broadcast_compare_fusion
  9.3 50.7 %all-gather.2.cloned.1.call-done = bf16[3,256,2048]{1,2,0:T(8,128)(2,1)} async-done(((bf16[3,128,2048]{1,2,0:T(8,128)(2,1)}), bf16[3,256,2048]{1,2,0:T(8,128)(2,1)}) %all-gather.2.cloned.1.call-update) | async-done | bytes 3145744 | tf_op jit(solution)/shard_map/all_gather | solution.py:115
  60.0 3.5 copy.51
  63.5 145.9 %while.18 = (s32[]{:T(128)}, f32[1,3,256,16]{2,3,1,0:T(8,128)S(1)}, f32[1,3,256,16]{2,3,1,0:T(8,128)S(1)}, f32[1,3,256,16,128]{4,2,3,1,0:T(8,128)}, bf16[2,2048,...) while((s32[]{:T(128)}, f32[1,3,256,16]{2,3,1,0:T(8,128)S(1)}, ...), condition=%wide.region_3.0_spmd.clone, body=%wide.region_0.0_spmd.clone.sunk | while | flops 3276349440 | bytes 92274880 | solution.py:61
  63.5 11.0 %bitcast_reduce_fusion.2 = (f32[3,256,16]{1,2,0:T(8,128)S(1)}, f32[512,3,256,16]{2,0,3,1:T(8,128)}) fusion(bf16[1,3,256,16,128]{4,2,3,1,0:T(8,128)(2,1)S(1)} %get-tuple-element.260, bf16[2,2048,128]{2,1,0:T(8,128)(2,1)} %get-tuple-element.259, s32[]{:T(128)S(6)} %select_n.47), kind=kOutput, calls=%fused_computation.1.clone.1 | convolution fusion | flops 1623183360 | bytes 28491780 | tf_op jit(solution)/shard_map/while/body/eval_jaxpr/hsiad,nhd->hsian/dot_general | solution.py:48
  74.5 10.5 %fusion.69 = f32[3,256,16]{1,2,0:T(8,128)S(1)} fusion(f32[512,3,256,16]{2,0,3,1:T(8,128)} %get-tuple-element.231, f32[3,256,16]{1,2,0:T(8,128)S(1)} %bitcast.201), kind=kLoop, calls=%fused_computation.4.clone.1 | loop fusion | flops 18862080 | bytes 25264128 | tf_op jit(solution)/shard_map/while/body/eval_jaxpr/reduce_sum | solution.py:33
  85.0 12.8 %bitcast_add_fusion.9 = f32[1,3,256,16,128]{4,2,3,1,0:T(8,128)} fusion(f32[1,3,256,16,128]{4,2,3,1,0:T(8,128)} %get-tuple-element.247, f32[3,256,16]{1,2,0:T(8,128)S(1)} %get-tuple-element.232, pred[]{:T(512)S(6)} %compare.3, f32[512,3,256,16]{2,0,3,1:T(8,128)} %get-tuple-element.231, f32[3,256,16]{1,2,0:T(8,128)S(1)} %bitcast.202, ...), kind=kOutput, calls=%fused_computation.8.clone.1 | convolution fusion | flops 1634205696 | bytes 37978120 | tf_op jit(solution)/shard_map/while/body/eval_jaxpr/hsian,nhd->hsiad/dot_general | solution.py:55
  97.8 11.0 %bitcast_reduce_fusion.2 = (f32[3,256,16]{1,2,0:T(8,128)S(1)}, f32[512,3,256,16]{2,0,3,1:T(8,128)}) fusion(bf16[1,3,256,16,128]{4,2,3,1,0:T(8,128)(2,1)S(1)} %get-tuple-element.260, bf16[2,2048,128]{2,1,0:T(8,128)(2,1)} %get-tuple-element.259, s32[]{:T(128)S(6)} %select_n.47), kind=kOutput, calls=%fused_computation.1.clone.1 | convolution fusion | flops 1623183360 | bytes 28491780 | tf_op jit(solution)/shard_map/while/body/eval_jaxpr/hsiad,nhd->hsian/dot_general | solution.py:48
  108.8 10.5 %fusion.69 = f32[3,256,16]{1,2,0:T(8,128)S(1)} fusion(f32[512,3,256,16]{2,0,3,1:T(8,128)} %get-tuple-element.231, f32[3,256,16]{1,2,0:T(8,128)S(1)} %bitcast.201), kind=kLoop, calls=%fused_computation.4.clone.1 | loop fusion | flops 18862080 | bytes 25264128 | tf_op jit(solution)/shard_map/while/body/eval_jaxpr/reduce_sum | solution.py:33
  119.3 15.7 %bitcast_add_fusion.9 = f32[1,3,256,16,128]{4,2,3,1,0:T(8,128)} fusion(f32[1,3,256,16,128]{4,2,3,1,0:T(8,128)} %get-tuple-element.247, f32[3,256,16]{1,2,0:T(8,128)S(1)} %get-tuple-element.232, pred[]{:T(512)S(6)} %compare.3, f32[512,3,256,16]{2,0,3,1:T(8,128)} %get-tuple-element.231, f32[3,256,16]{1,2,0:T(8,128)S(1)} %bitcast.202, ...), kind=kOutput, calls=%fused_computation.8.clone.1 | convolution fusion | flops 1634205696 | bytes 37978120 | tf_op jit(solution)/shard_map/while/body/eval_jaxpr/hsian,nhd->hsiad/dot_general | solution.py:55
  135.0 11.0 %bitcast_reduce_fusion.2 = (f32[3,256,16]{1,2,0:T(8,128)S(1)}, f32[512,3,256,16]{2,0,3,1:T(8,128)}) fusion(bf16[1,3,256,16,128]{4,2,3,1,0:T(8,128)(2,1)S(1)} %get-tuple-element.260, bf16[2,2048,128]{2,1,0:T(8,128)(2,1)} %get-tuple-element.259, s32[]{:T(128)S(6)} %select_n.47), kind=kOutput, calls=%fused_computation.1.clone.1 | convolution fusion | flops 1623183360 | bytes 28491780 | tf_op jit(solution)/shard_map/while/body/eval_jaxpr/hsiad,nhd->hsian/dot_general | solution.py:48
  146.0 10.5 %fusion.69 = f32[3,256,16]{1,2,0:T(8,128)S(1)} fusion(f32[512,3,256,16]{2,0,3,1:T(8,128)} %get-tuple-element.231, f32[3,256,16]{1,2,0:T(8,128)S(1)} %bitcast.201), kind=kLoop, calls=%fused_computation.4.clone.1 | loop fusion | flops 18862080 | bytes 25264128 | tf_op jit(solution)/shard_map/while/body/eval_jaxpr/reduce_sum | solution.py:33
  156.5 15.7 %bitcast_add_fusion.9 = f32[1,3,256,16,128]{4,2,3,1,0:T(8,128)} fusion(f32[1,3,256,16,128]{4,2,3,1,0:T(8,128)} %get-tuple-element.247, f32[3,256,16]{1,2,0:T(8,128)S(1)} %get-tuple-element.232, pred[]{:T(512)S(6)} %compare.3, f32[512,3,256,16]{2,0,3,1:T(8,128)} %get-tuple-element.231, f32[3,256,16]{1,2,0:T(8,128)S(1)} %bitcast.202, ...), kind=kOutput, calls=%fused_computation.8.clone.1 | convolution fusion | flops 1634205696 | bytes 37978120 | tf_op jit(solution)/shard_map/while/body/eval_jaxpr/hsian,nhd->hsiad/dot_general | solution.py:55
  172.2 11.0 %bitcast_reduce_fusion.2 = (f32[3,256,16]{1,2,0:T(8,128)S(1)}, f32[512,3,256,16]{2,0,3,1:T(8,128)}) fusion(bf16[1,3,256,16,128]{4,2,3,1,0:T(8,128)(2,1)S(1)} %get-tuple-element.260, bf16[2,2048,128]{2,1,0:T(8,128)(2,1)} %get-tuple-element.259, s32[]{:T(128)S(6)} %select_n.47), kind=kOutput, calls=%fused_computation.1.clone.1 | convolution fusion | flops 1623183360 | bytes 28491780 | tf_op jit(solution)/shard_map/while/body/eval_jaxpr/hsiad,nhd->hsian/dot_general | solution.py:48
  183.2 10.5 %fusion.69 = f32[3,256,16]{1,2,0:T(8,128)S(1)} fusion(f32[512,3,256,16]{2,0,3,1:T(8,128)} %get-tuple-element.231, f32[3,256,16]{1,2,0:T(8,128)S(1)} %bitcast.201), kind=kLoop, calls=%fused_computation.4.clone.1 | loop fusion | flops 18862080 | bytes 25264128 | tf_op jit(solution)/shard_map/while/body/eval_jaxpr/reduce_sum | solution.py:33
  193.7 15.7 %bitcast_add_fusion.9 = f32[1,3,256,16,128]{4,2,3,1,0:T(8,128)} fusion(f32[1,3,256,16,128]{4,2,3,1,0:T(8,128)} %get-tuple-element.247, f32[3,256,16]{1,2,0:T(8,128)S(1)} %get-tuple-element.232, pred[]{:T(512)S(6)} %compare.3, f32[512,3,256,16]{2,0,3,1:T(8,128)} %get-tuple-element.231, f32[3,256,16]{1,2,0:T(8,128)S(1)} %bitcast.202, ...), kind=kOutput, calls=%fused_computation.8.clone.1 | convolution fusion | flops 1634205696 | bytes 37978120 | tf_op jit(solution)/shard_map/while/body/eval_jaxpr/hsian,nhd->hsiad/dot_general | solution.py:55
  209.4 9.2 %copy.55 = f32[1,3,256,16,128]{4,3,1,2,0:T(8,128)} copy(f32[1,3,256,16,128]{4,2,3,1,0:T(8,128)} %get-tuple-element.116) | data formatting | bytes 12582912 | tf_op jit(solution)/shard_map/while | solution.py:61
  218.6 0.0 copy-done
  218.6 0.3 constant_dynamic-slice_fusion
  219.0 1.7 copy.54
  220.7 0.2 copy.53
  220.9 0.0 copy-start.5
  220.9 0.8 copy.92
  221.8 0.2 copy-done.5
  221.9 1.0 copy.60
  223.0 5.8 %fusion.27 = (f32[3,128,16]{2,0,1:T(4,128)S(1)}, f32[128,3,16,128]{3,2,1,0:T(8,128)S(1)}) fusion(pred[128,128]{1,0:T(8,128)(4,1)S(1)} %broadcast_compare_fusion, bf16[2,128,128,128]{3,2,1,0:T(8,128)(2,1)} %param.10, bf16[1,3,128,16,128]{4,3,1,2,0:T(8,128)(2,1)} %copy.54), kind=kOutput, calls=%fused_computation.39 | convolution fusion | flops 203679744 | bytes 8953856 | tf_op jit(solution)/shard_map/hsiad,inhd->hsian/dot_general | solution.py:71
  228.8 1.7 constant_dynamic-update-slice_fusion
  230.6 57.2 %pmax.7 = f32[1,3,256,16]{3,1,2,0:T(4,128)} all-reduce(f32[1,3,256,16]{3,1,2,0:T(4,128)} %get-tuple-element.172), channel_id=1, replica_groups=mesh['group'=2,'seq'=8,'head'=8] {'group','seq'}, use_global_device_ids=true, to_apply=%region_5.6 | all-reduce | flops 12288 | bytes 98304 | tf_op jit(solution)/shard_map/pmax | solution.py:135
  287.8 1.9 fusion.25
  289.6 0.0 copy-done.4
  289.7 0.0 copy-done.6
  289.7 0.2 fusion.54
  289.9 5.3 %fusion.23 = f32[1,3,256,16,128]{4,3,1,2,0:T(8,128)} fusion(f32[1,3,256,16,128]{4,3,1,2,0:T(8,128)} %copy.55, s32[]{:T(128)S(6)} %select_n.28, bf16[2,128,128,128]{3,2,1,0:T(8,128)(2,1)} %param.10, f32[128,3,16,128]{3,2,1,0:T(8,128)S(1)} %get-tuple-element.185, f32[3,128,16]{2,0,1:T(4,128)S(1)} %bitcast.207, f32[3,128,16]{2,0,1:T(4,128)S(1)} %get-tuple-element.181, ...), kind=kOutput, calls=%fused_computation.32 | convolution fusion | flops 206045184 | bytes 13697028 | tf_op jit(solution)/shard_map/hsian,inhd->hsiad/dot_general | solution.py:79
  295.2 0.0 copy-done.2
  295.2 1.3 fusion.56
  296.5 7.4 %broadcast_multiply_fusion = f32[1,3,256,16,128]{4,3,1,2,0:T(8,128)} fusion(f32[1,3,256,16,128]{4,3,1,2,0:T(8,128)} %fusion.23, f32[3,256,16]{2,0,1:T(4,128)S(1)} %get-tuple-element.177), kind=kLoop, calls=%fused_computation.35 | loop fusion | flops 1572864 | bytes 12632064 | tf_op jit(solution)/shard_map/mul | solution.py:139
  303.9 0.0 reduce-scatter.2.cloned.1.call-update
  303.9 0.0 copy-start.10
  304.0 0.0 copy-start.8
  304.0 0.0 all-reduce.3.cloned.1.call-start
  304.0 82.5 %reduce-scatter.2.cloned.1.call-done = f32[1,3,128,16,128]{4,3,1,2,0:T(8,128)} async-done(((f32[1,3,256,16,128]{4,3,1,2,0:T(8,128)}), f32[1,3,128,16,128]{4,3,1,2,0:T(8,128)}) %reduce-scatter.2.cloned.1.call-update) | async-done | bytes 3145744 | tf_op jit(solution)/shard_map/reduce_scatter | solution.py:139
  386.5 0.0 all-reduce.3.cloned.1.call-update
  386.6 0.6 dynamic-slice
  387.8 0.0 copy-start.3
  387.8 0.4 copy.61
  388.2 11.3 %all-reduce = f32[1,3,256,16]{3,0,1,2:T(1,128)S(1)} all-reduce(f32[1,3,256,16]{3,0,1,2:T(1,128)S(1)} %copy.61), channel_id=3, replica_groups=mesh['group'=2,'seq'=8,'head'=8] {'group'}, use_global_device_ids=true, to_apply=%region_10.11.clone | all-reduce | flops 12288 | bytes 98304
  399.5 0.1 constant_dynamic-slice_fusion.1
  399.6 26.9 %psum.15 = f32[1,3,128,16]{3,1,2,0:T(4,128)S(1)} all-reduce(f32[1,3,128,16]{3,1,2,0:T(4,128)S(1)} %copy.62), channel_id=1, replica_groups=mesh['group'=2,'seq'=8,'head'=8] {'seq'}, use_global_device_ids=true, to_apply=%region_11.12 | all-reduce | flops 6144 | bytes 49152 | tf_op jit(solution)/shard_map/psum | solution.py:141
  426.6 0.0 copy-done.1
  426.6 3.0 fusion.63
  429.6 0.0 copy-start.7
  429.6 0.1 fusion.55
  429.7 0.8 copy-done.7
  430.5 0.7 fusion.48
  431.2 0.2 fusion.59
  431.4 27.0 %all-reduce.3.cloned.1.call-done = f32[1,3,128,16,128]{4,3,1,2,0:T(8,128)} async-done(((f32[1,3,128,16,128]{4,3,1,2,0:T(8,128)}), f32[1,3,128,16,128]{4,3,1,2,0:T(8,128)}) %all-reduce.3.cloned.1.call-update) | async-done | bytes 3145744 | tf_op jit(solution)/shard_map/psum | solution.py:141
  458.4 4.1 fusion.22
  462.4 1.3 copy.63
  463.7 1.6 copy.64
  (28 shorter events, 0.3 us)
Async XLA Ops:
  6.5 2.7 copy-start.9
  6.5 53.5 %all-gather.2.cloned.1.call-start = ((), (), s32[]{:S(2)}) async-start(), calls=%async_computation.1 | async-start | bytes 4718592 | tf_op jit(solution)/shard_map/all_gather | solution.py:115
  9.1 377.4 %reduce-scatter.2.cloned.1.call-start = ((), (), s32[]{:S(2)}) async-start(), calls=%async_computation.2 | async-start | bytes 9437184 | tf_op jit(solution)/shard_map/reduce_scatter | solution.py:139
  209.4 9.2 %copy-start = (bf16[3,256,2048]{1,2,0:T(8,128)(2,1)S(1)}, bf16[3,256,2048]{1,2,0:T(8,128)(2,1)}, u32[]{:S(2)}) copy-start(bf16[3,256,2048]{1,2,0:T(8,128)(2,1)} %all-gather.2.cloned.1.call-done) | copy-start | bytes 9437188
  220.9 1.0 copy-start.5
  287.7 1.9 copy-start.4
  287.7 1.9 copy-start.6
  289.9 5.3 %copy-start.2 = (f32[1,3,256,16]{3,1,2,0:T(4,128)S(1)}, f32[1,3,256,16]{3,1,2,0:T(4,128)}, u32[]{:S(2)}) copy-start(f32[1,3,256,16]{3,1,2,0:T(4,128)} %pmax.7) | copy-start | bytes 147460
  303.9 82.6 %copy-start.10 = (u32[128]{0:T(128)S(1)}, u32[128]{0:T(128)}, u32[]{:S(2)}) copy-start(u32[128]{0:T(128)} %constant.77) | copy-start | bytes 1540
  304.0 83.8 %copy-start.8 = (bf16[2,3,128,128]{3,2,1,0:T(8,128)(2,1)S(1)}, bf16[2,3,128,128]{3,2,1,0:T(8,128)(2,1)}, u32[]{:S(2)}) copy-start(bf16[2,3,128,128]{3,2,1,0:T(8,128)(2,1)} %param.9) | copy-start | bytes 589828
  304.0 154.4 %all-reduce.3.cloned.1.call-start = ((), (), s32[]{:S(2)}) async-start(), calls=%async_computation.3 | async-start | bytes 6291456 | tf_op jit(solution)/shard_map/psum | solution.py:141
  386.5 40.0 %copy-start.1 = (bf16[1,3,128,16,128]{4,3,1,2,0:T(8,128)(2,1)S(1)}, bf16[1,3,128,16,128]{4,3,1,2,0:T(8,128)(2,1)}, u32[]{:S(2)}) copy-start(bf16[1,3,128,16,128]{4,3,1,2,0:T(8,128)(2,1)} %copy.54) | copy-start | bytes 4718596
  387.8 41.8 %copy-start.3 = (f32[1,3,256,16]{3,1,2,0:T(4,128)S(1)}, f32[1,3,256,16]{3,1,2,0:T(4,128)}, u32[]{:S(2)}) copy-start(f32[1,3,256,16]{3,1,2,0:T(4,128)} %pmax.7) | copy-start | bytes 147460
  429.6 0.9 copy-start.7
Sparse Core Ops, SparseCore 0:
  9.3 50.6 all-gather.1
  304.1 82.4 reduce-scatter.1
  389.0 69.2 all-reduce.2
where the time goes:
time: 474 us; the launch traced here: 472 us
  waiting for transfers between devices  160 us (34%)
  matrix products  122 us (26%)
  blocking collectives  95.4 us (20%)
  other arithmetic  55.7 us (12%)
  local copies, waits for them, and re-layouts  24.4 us (5%)
  between operations  14 us (3%)
    reduce_scatter x1, waiting for transfers between devices, local(): lax.psum_scatter(local_out * rate[..., None], 'group', scatter_dimension=...  82.5 us
    dot_general x4, matrix products, mix_values(): jnp.einsum('hsian,nhd->hsiad', weights, value_block, preferred_element_ty...  59.8 us
    pmax x1, blocking collectives, local(): global_max = lax.pmax(local_max, ('group', 'seq'))  57.2 us
    all_gather x1, waiting for transfers between devices, local(): everyone = lax.all_gather(queries, 'group', axis=1, tiled=True)  50.7 us
    reduce_sum x6, other arithmetic, absorb(): running_sum = running_sum * rescale + jnp.sum(weights, axis=-1)  44.5 us
    dot_general x4, matrix products, one_block(): jnp.einsum('hsiad,nhd->hsian', query_heads, key_block, preferred_element_...  43.8 us
    psum x1, waiting for transfers between devices, local(): summed = lax.psum((shares[0], shares[1]), 'seq')  27 us
    psum x1, blocking collectives, local(): summed = lax.psum((shares[0], shares[1]), 'seq')  26.9 us
  transfers between devices with their start and end apart: 3, of which 3 were waited for; matrix products, arithmetic and copies ran while one was open for 1% of the time, Pallas kernels for 0%

commit v1 on v0

v1 whole, which is shorter than its diff:
```python
import jax
import jax.numpy as jnp
from jax import lax
from jax.experimental import pallas as pl
from jax.experimental.pallas import tpu as pltpu
from jax.sharding import PartitionSpec as P

DH = 128
STEPS = 3
MASKED_SCORE = -1e30
LOG2E = 1.4426950408889634
SCALE = LOG2E * DH**-0.5
MESH = pl.DeviceIdType.MESH

ROW_TILE = 1024
TOKEN_BLOCK = 256
PIECE = 128
EXTRA = 16
HI, LO = jnp.float32, jnp.bfloat16


def dot_nt(a, b):
    return lax.dot_general(a, b, (((1,), (1,)), ((), ())), preferred_element_type=HI)


def dot_nn(a, b):
    return lax.dot_general(a, b, (((1,), (0,)), ((), ())), preferred_element_type=HI)


def twice(a):
    return jnp.concatenate([a, a], axis=1)


def with_ones(values):
    return jnp.concatenate([values, jnp.ones_like(values)], axis=1)


def absorb(scores, values, state_max, state_out):
    width = scores.shape[1]
    new_max = jnp.maximum(state_max, jnp.max(scores, axis=1, keepdims=True))
    weights = jnp.exp2(scores - jnp.concatenate([new_max] * (width // DH), axis=1))
    mixed = dot_nn(weights.astype(LO), with_ones(values))
    if state_out is not None:
        mixed = state_out * twice(jnp.exp2(state_max - new_max)) + mixed
    return new_max, mixed


def encode_logsum(logsum):
    flat = jnp.transpose(logsum)[0:EXTRA]
    high = flat.astype(LO).astype(HI)
    middle = (flat - high).astype(LO).astype(HI)
    low = flat - high - middle
    row = lax.broadcasted_iota(jnp.int32, (EXTRA, DH), 0)
    return jnp.where(
        row == 0, high, jnp.where(row == 1, middle, jnp.where(row == 2, low, 0.0))
    ).astype(LO)


def decode_logsum(coded):
    parts = coded.astype(HI)
    flat = parts[0:1] + parts[1:2] + parts[2:3]
    return jnp.transpose(jnp.broadcast_to(flat, (PIECE, DH)))


def merge(pieces):
    logsums = [decode_logsum(p[PIECE:]) for p in pieces]
    top = logsums[0]
    for logsum in logsums[1:]:
        top = jnp.maximum(top, logsum)
    shares = [jnp.exp2(logsum - top) for logsum in logsums]
    total = sum(shares[1:], shares[0])
    mixed = None
    for share, piece in zip(shares, pieces):
        term = share * piece[:PIECE].astype(HI)
        mixed = term if mixed is None else mixed + term
    return mixed / total, top + jnp.log(total) * LOG2E


def kernel(
    lengths_ref, prompt_ref, query_ref, new_ref, resident_ref, out_ref,
    own, far, wide, resident, fresh, state_max, state_out,
    part, swapped, joined, crossed,
    local_sems, resident_sems, far_send, far_recv, swap_send, swap_recv,
    cross_send, cross_recv, gather_send, gather_recv, forward_send, forward_recv,
):
    rows = query_ref.shape[0]
    samples = lengths_ref.shape[0]
    blocks = rows // ROW_TILE
    per_sample = rows // samples
    slots = resident_ref.shape[2]
    tokens = prompt_ref.shape[1]
    group = lax.axis_index("group")
    seq = lax.axis_index("seq")
    x, core = seq // 2, lax.rem(seq, 2)
    other_group = {"group": 1 - group}
    other_core = {"seq": 2 * x + 1 - core}
    peers = [lax.rem(x + d, 4) for d in (1, 2, 3)]
    sources = [lax.rem(x + 4 - d, 4) for d in (1, 2, 3)]

    barrier = pltpu.get_barrier_semaphore()
    greeted = [other_group, other_core] + [{"seq": 2 * p + core} for p in peers]
    for device in greeted:
        pl.semaphore_signal(barrier, inc=1, device_id=device, device_id_type=MESH)

    prompt_copy = pltpu.make_async_copy(prompt_ref, own, local_sems.at[0])
    prompt_copy.start()
    fresh_copies = [
        pltpu.make_async_copy(
            new_ref.at[kind, :, pl.ds(pl.multiple_of(seq * 16, 16), 16)],
            fresh.at[kind],
            local_sems.at[1 + kind],
        )
        for kind in (0, 1)
    ]
    for copy in fresh_copies:
        copy.start()
    chunks = resident_sems.shape[0]
    chunk = samples // chunks

    def resident_copy(index):
        return pltpu.make_async_copy(
            resident_ref.at[:, pl.ds(index * chunk, chunk)],
            resident.at[:, pl.ds(index * chunk, chunk)],
            resident_sems.at[index],
        )

    for index in range(chunks):
        resident_copy(index).start()

    pl.semaphore_wait(barrier, len(greeted))
    far_copies = [
        pltpu.make_async_remote_copy(
            src_ref=prompt_ref.at[kind],
            dst_ref=far.at[kind],
            send_sem=far_send.at[kind],
            recv_sem=far_recv.at[kind],
            device_id=other_group,
            device_id_type=MESH,
        )
        for kind in (0, 1)
    ]
    for copy in far_copies:
        copy.start()

    def widen(index, carry):
        at = pl.ds(pl.multiple_of(index * 512, 512), 512)
        scaled = query_ref[at].astype(HI) * SCALE
        high = scaled.astype(LO)
        wide[at] = jnp.concatenate([high, (scaled - high.astype(HI)).astype(LO)], axis=1)
        return carry

    lax.fori_loop(0, rows // 512, widen, 0)
    prompt_copy.wait()

    def prompt_tile(at, source, first):
        queries = wide[at]
        top = jnp.full((ROW_TILE, DH), MASKED_SCORE, HI) if first else state_max[at]
        mixed = None if first else state_out[at]
        for start in range(0, tokens, TOKEN_BLOCK):
            span = pl.ds(start, TOKEN_BLOCK)
            scores = dot_nt(queries, twice(source[0, span]))
            top, mixed = absorb(scores, source[1, span], top, mixed)
        return top, mixed

    def tile_rows(index):
        return pl.ds(pl.multiple_of(index * ROW_TILE, ROW_TILE), ROW_TILE)

    def own_tile(index, carry):
        at = tile_rows(index)
        state_max[at], state_out[at] = prompt_tile(at, own, True)
        return carry

    lax.fori_loop(0, blocks, own_tile, 0)

    for copy in fresh_copies:
        copy.wait()
    new_rows = 16 * per_sample
    at = pl.ds(pl.multiple_of(seq * new_rows, new_rows), new_rows)
    padding = jnp.zeros((DH - STEPS * 16, DH), LO)
    new_keys = jnp.concatenate([fresh[0, t] for t in range(STEPS)] + [padding], axis=0)
    new_values = jnp.concatenate([fresh[1, t] for t in range(STEPS)] + [padding], axis=0)
    scores = dot_nt(wide[at], twice(new_keys))
    row = lax.broadcasted_iota(jnp.int32, scores.shape, 0)
    column = lax.broadcasted_iota(jnp.int32, scores.shape, 1)
    row_sample = row // per_sample
    row_step = (row - row_sample * per_sample) // (per_sample // STEPS)
    seen = (column // 16 <= row_step) & (lax.rem(column, 16) == row_sample)
    scores = jnp.where(seen, scores, MASKED_SCORE)
    state_max[at], state_out[at] = absorb(scores, new_values, state_max[at], state_out[at])

    pair_rows = 2 * per_sample
    row = lax.broadcasted_iota(jnp.int32, (pair_rows, 2 * slots), 0)
    column = lax.broadcasted_iota(jnp.int32, (pair_rows, 2 * slots), 1)
    is_first = row < per_sample
    begin = jnp.where(is_first, 0, slots)

    def resident_pair(index):
        first = 2 * index
        at = pl.ds(pl.multiple_of(index * pair_rows, 32), pair_rows)
        pair = pl.ds(first, 2)
        keys = resident[0, pair].reshape(2 * slots, DH)
        values = resident[1, pair].reshape(2 * slots, DH)
        scores = dot_nt(wide[at], twice(keys))
        here = seq * slots
        one = jnp.minimum(lengths_ref[first] - here, slots)
        two = jnp.minimum(lengths_ref[first + 1] - here, slots) + slots
        seen = (column >= begin) & (column < jnp.where(is_first, one, two))
        scores = jnp.where(seen, scores, MASKED_SCORE)
        return at, absorb(scores, values, state_max[at], state_out[at])

    def resident_step(index, carry):
        results = [resident_pair(index * 4 + u) for u in range(4)]
        for at, (top, mixed) in results:
            state_max[at] = top
            state_out[at] = mixed
        return carry

    steps_per_chunk = chunk // 8
    for index in range(chunks):
        resident_copy(index).wait()
        lax.fori_loop(index * steps_per_chunk, (index + 1) * steps_per_chunk, resident_step, 0)

    for copy in far_copies:
        copy.wait_recv()

    def swap_copy(b):
        return pltpu.make_async_remote_copy(
            src_ref=part.at[b, 1 - core], dst_ref=swapped.at[b],
            send_sem=swap_send.at[b], recv_sem=swap_recv.at[b],
            device_id=other_core, device_id_type=MESH,
        )

    def cross_copy(b, d):
        return pltpu.make_async_remote_copy(
            src_ref=joined.at[b, peers[d]], dst_ref=crossed.at[b, d],
            send_sem=cross_send.at[b, d], recv_sem=cross_recv.at[b, d],
            device_id={"seq": 2 * peers[d] + core}, device_id_type=MESH,
        )

    def piece_rows(b, owner):
        start = b * ROW_TILE + core * (ROW_TILE // 2) + owner * PIECE
        return pl.ds(pl.multiple_of(start, PIECE), PIECE)

    def gather_copy(b, d, owner):
        at = piece_rows(b, owner)
        return pltpu.make_async_remote_copy(
            src_ref=out_ref.at[at], dst_ref=out_ref.at[at],
            send_sem=gather_send.at[b, d], recv_sem=gather_recv.at[b, d],
            device_id={"seq": 2 * peers[d] + core}, device_id_type=MESH,
        )

    def forward_copy(b, half):
        start = b * ROW_TILE + half * (ROW_TILE // 2)
        at = pl.ds(pl.multiple_of(start, ROW_TILE // 2), ROW_TILE // 2)
        return pltpu.make_async_remote_copy(
            src_ref=out_ref.at[at], dst_ref=out_ref.at[at],
            send_sem=forward_send.at[b], recv_sem=forward_recv.at[b],
            device_id=other_core, device_id_type=MESH,
        )

    def far_tile(b):
        top, mixed = prompt_tile(tile_rows(b), far, False)
        total = mixed[:, DH:]
        mean = (mixed[:, :DH] / total).astype(LO)
        logsum = top + jnp.log(total) * LOG2E
        for index in range(ROW_TILE // PIECE):
            span = slice(index * PIECE, (index + 1) * PIECE)
            half, owner = index // 4, index % 4
            part[b, half, owner, 0:PIECE] = mean[span]
            part[b, half, owner, PIECE:] = encode_logsum(logsum[span])
        swap_copy(b).start()

    def join_cores(b):
        swap_copy(b).wait_recv()
        for owner in range(4):
            mean, logsum = merge([part[b, core, owner], swapped[b, owner]])
            joined[b, owner, 0:PIECE] = mean.astype(LO)
            joined[b, owner, PIECE:] = encode_logsum(logsum)
        for d in range(3):
            cross_copy(b, d).start()

    def join_chips(b):
        for d in range(3):
            cross_copy(b, d).wait_recv()
        mean, _ = merge([joined[b, x]] + [crossed[b, d] for d in range(3)])
        out_ref[piece_rows(b, x)] = mean.astype(LO)
        for d in range(3):
            gather_copy(b, d, x).start()

    def forward(b):
        for d in range(3):
            gather_copy(b, d, sources[d]).wait_recv()
        forward_copy(b, core).start()

    def turn(b, carry):
        pl.when(b < blocks)(lambda: far_tile(b))
        pl.when((b >= 1) & (b < blocks + 1))(lambda: join_cores(b - 1))
        pl.when((b >= 2) & (b < blocks + 2))(lambda: join_chips(b - 2))
        pl.when(b >= 3)(lambda: forward(b - 3))
        return carry

    lax.fori_loop(0, blocks + 3, turn, 0)

    for copy in far_copies:
        copy.wait_send()

    def finish(b, carry):
        swap_copy(b).wait_send()
        for d in range(3):
            cross_copy(b, d).wait_send()
            gather_copy(b, d, x).wait_send()
        forward_copy(b, core).wait_send()
        forward_copy(b, 1 - core).wait_recv()
        return carry

    lax.fori_loop(0, blocks, finish, 0)


def local(prompt_kv, queries, new_kv, resident_kv, seq_lengths):
    steps, samples, columns = queries.shape
    heads = columns // DH
    rows = steps * samples * heads
    query_rows = jnp.transpose(queries.reshape(steps, samples, heads, DH), (1, 0, 2, 3))
    query_rows = query_rows.reshape(rows, DH)
    blocks = rows // ROW_TILE
    piece = (PIECE + EXTRA, DH)
    dma = pltpu.SemaphoreType.DMA
    anywhere = pl.BlockSpec(memory_space=pl.ANY)
    in_vmem = pl.BlockSpec(memory_space=pltpu.VMEM)
    out = pl.pallas_call(
        kernel,
        out_shape=jax.ShapeDtypeStruct((rows, DH), LO),
        in_specs=[pl.BlockSpec(memory_space=pltpu.SMEM), anywhere, in_vmem, anywhere, anywhere],
        out_specs=in_vmem,
        scratch_shapes=[
            pltpu.VMEM(prompt_kv.shape, LO),
            pltpu.VMEM(prompt_kv.shape, LO),
            pltpu.VMEM((rows, 2 * DH), LO),
            pltpu.VMEM(resident_kv.shape, LO),
            pltpu.VMEM((2, steps, 16, DH), LO),
            pltpu.VMEM((rows, DH), HI),
            pltpu.VMEM((rows, 2 * DH), HI),
            pltpu.VMEM((blocks, 2, 4) + piece, LO),
            pltpu.VMEM((blocks, 4) + piece, LO),
            pltpu.VMEM((blocks, 4) + piece, LO),
            pltpu.VMEM((blocks, 3) + piece, LO),
            dma((3,)), dma((4,)), dma((2,)), dma((2,)), dma((blocks,)), dma((blocks,)),
            dma((blocks, 3)), dma((blocks, 3)), dma((blocks, 3)), dma((blocks, 3)),
            dma((blocks,)), dma((blocks,)),
        ],
        compiler_params=pltpu.CompilerParams(
            collective_id=0, has_side_effects=True, vmem_limit_bytes=58 * 2**20
        ),
    )(seq_lengths, prompt_kv, query_rows, new_kv, resident_kv)
    out = jnp.transpose(out.reshape(samples, steps, heads, DH), (1, 0, 2, 3))
    return out.reshape(queries.shape)


def solution(mesh):
    placed = (
        P(None, ("group", "seq"), "head"),
        P(None, "group", "head"),
        P(None, None, "group", "head"),
        P(None, "group", "seq", "head"),
        P("group"),
    )
    return jax.shard_map(
        local, mesh=mesh, in_specs=placed, out_specs=P(None, "group", "head"), check_vma=False
    )
```

time: 474 us -> 87.6 us (0.18)
  waiting for transfers between devices: 160 us -> 0 us
  matrix products: 122 us -> 0 us
  blocking collectives: 95.4 us -> 0 us
  Pallas kernels: 0 us -> 80.5 us
  other arithmetic: 55.7 us -> 0 us
  local copies, waits for them, and re-layouts: 24.4 us -> 6.96 us
  between operations: 14 us -> 0.02 us
    dot_general x12 -> x0, matrix products: 122 us -> none  [the longest x4 59.8 us: mix_values(): jnp.einsum('hsian,nhd->hsiad', weights, value_block, preferred_element_ty...]
    reduce_scatter x1 -> x0, waiting for transfers between devices: 82.5 us -> none  [local(): lax.psum_scatter(local_out * rate[..., None], 'group', scatter_dimension=...]
    pallas_call x0 -> x1, Pallas kernels: none -> 80.5 us  [local(): pl.pallas_call(kernel, out_shape=jax.ShapeDtypeStruct((rows, DH), LO), in...]
    pmax x1 -> x0, blocking collectives: 57.2 us -> none  [local(): global_max = lax.pmax(local_max, ('group', 'seq'))]
    all_gather x1 -> x0, waiting for transfers between devices: 50.7 us -> none  [local(): everyone = lax.all_gather(queries, 'group', axis=1, tiled=True)]
    reduce_sum x6 -> x0, other arithmetic: 44.5 us -> none  [absorb(): running_sum = running_sum * rescale + jnp.sum(weights, axis=-1)]
    psum x1 -> x0, waiting for transfers between devices: 27 us -> none  [local(): summed = lax.psum((shares[0], shares[1]), 'seq')]
    psum x1 -> x0, blocking collectives: 26.9 us -> none  [local(): summed = lax.psum((shares[0], shares[1]), 'seq')]
  transfers between devices with their start and end apart: 3 -> 0, of which waited for: 3 -> 0; matrix products, arithmetic and copies ran while one was open for 1% -> 0% of each run, Pallas kernels for 0% -> 0%
where the time goes in v1:
time: 87.6 us; the launch traced here: 87.4 us
  Pallas kernels  80.5 us (92%)
  local copies, waits for them, and re-layouts  6.96 us (8%)
    pallas_call x1, Pallas kernels, local(): pl.pallas_call(kernel, out_shape=jax.ShapeDtypeStruct((rows, DH), LO), in...  80.5 us
    reshape x1, local copies, waits for them, and re-layouts, local(): return out.reshape(queries.shape)  2.06 us
    unnamed x1, local copies, waits for them, and re-layouts  1.81 us

profile of v1, /device:TPU:1, one launch (start us, length us, event | category | flops | bytes accessed | tf_op | source)
XLA Modules:
  0.0 87.4 jit_solution(5598981571551465500)
XLA Ops:
  0.0 1.8 %copy.8 = bf16[48,8,16,128]{3,2,1,0:T(8,128)(2,1)S(1)} copy(bf16[48,8,16,128]{3,1,2,0:T(8,128)(2,1)} %bitcast.15) | data formatting | bytes 3145728
  1.8 1.4 %copy.6 = bf16[3,128,16,128]{3,2,0,1:T(8,128)(2,1)} copy(bf16[3,128,16,128]{3,2,1,0:T(8,128)(2,1)S(1)} %bitcast.14) | data formatting | bytes 3145728 | tf_op jit(solution)/shard_map/reshape | solution.py:323
  3.2 80.5 %shard_map.55 = bf16[6144,128]{1,0:T(8,128)(2,1)} custom-call(s32[128]{0:T(128)} %lengths_ref.1, bf16[2,2048,128]{2,1,0:T(8,128)(2,1)} %prompt_ref.1, bf16[6144,128]{1,0:T(8,128)(2,1)} %bitcast.12, bf16[2,3,128,128]{3,2,1,0:T(8,128)(2,1)} %new_ref.1, bf16[2,128,128,128]{3,2,1,0:T(8,128)(2,1)} %resident_ref.1), custom_call_target="tpu_custom_call" | custom-call | tf_op jit(solution)/shard_map/pallas_call | solution.py:330
  83.7 1.7 %copy.7 = bf16[3,128,16,128]{3,2,1,0:T(8,128)(2,1)S(1)} copy(bf16[3,128,16,128]{3,2,0,1:T(8,128)(2,1)} %bitcast.13) | data formatting | bytes 3145728 | tf_op jit(solution)/shard_map/transpose | solution.py:355
  85.4 2.1 %reshape.15 = bf16[3,128,2048]{2,1,0:T(8,128)(2,1)} reshape(bf16[3,128,16,128]{3,2,1,0:T(8,128)(2,1)S(1)} %copy.7) | data formatting | bytes 3145728 | tf_op jit(solution)/shard_map/reshape | solution.py:356

commit v2 on v1

--- a/solution.py
+++ b/solution.py
@@ -13,7 +13,10 @@
 MESH = pl.DeviceIdType.MESH
 
 ROW_TILE = 1024
-TOKEN_BLOCK = 256
+OWN_ROWS = 2048
+GROUP_ROWS = 256
+TOKEN_BLOCK = 1024
+LAGS = (1, 3, 5)
 PIECE = 128
 EXTRA = 16
 HI, LO = jnp.float32, jnp.bfloat16
@@ -77,16 +80,17 @@
 
 
 def kernel(
-    lengths_ref, prompt_ref, query_ref, new_ref, resident_ref, out_ref,
-    own, far, wide, resident, fresh, state_max, state_out,
+    lengths_ref, prompt_ref, asked_ref, new_ref, resident_ref, out_ref,
+    cached, asked, spread, query_ref, wide, resident, fresh, state_max, state_out,
     part, swapped, joined, crossed,
     local_sems, resident_sems, far_send, far_recv, swap_send, swap_recv,
     cross_send, cross_recv, gather_send, gather_recv, forward_send, forward_recv,
 ):
+    samples = lengths_ref.shape[0]
     rows = query_ref.shape[0]
-    samples = lengths_ref.shape[0]
     blocks = rows // ROW_TILE
-    per_sample = rows // samples
+    step_rows = rows // STEPS
+    heads = step_rows // samples
     slots = resident_ref.shape[2]
     tokens = prompt_ref.shape[1]
     group = lax.axis_index("group")
@@ -102,8 +106,12 @@
     for device in greeted:
         pl.semaphore_signal(barrier, inc=1, device_id=device, device_id_type=MESH)
 
-    prompt_copy = pltpu.make_async_copy(prompt_ref, own, local_sems.at[0])
+    prompt_copy = pltpu.make_async_copy(
+        prompt_ref, cached.at[:, pl.ds(0, tokens)], local_sems.at[0]
+    )
     prompt_copy.start()
+    asked_copy = pltpu.make_async_copy(asked_ref, asked, local_sems.at[3])
+    asked_copy.start()
     fresh_copies = [
         pltpu.make_async_copy(
             new_ref.at[kind, :, pl.ds(pl.multiple_of(seq * 16, 16), 16)],
@@ -127,11 +135,21 @@
     for index in range(chunks):
         resident_copy(index).start()
 
+    def tile_rows(index):
+        return pl.ds(pl.multiple_of(index * ROW_TILE, ROW_TILE), ROW_TILE)
+
+    def clear(index, carry):
+        state_max[tile_rows(index)] = jnp.full((ROW_TILE, DH), MASKED_SCORE, HI)
+        state_out[tile_rows(index)] = jnp.zeros((ROW_TILE, 2 * DH), HI)
+        return carry
+
+    lax.fori_loop(0, blocks, clear, 0)
+
     pl.semaphore_wait(barrier, len(greeted))
     far_copies = [
         pltpu.make_async_remote_copy(
             src_ref=prompt_ref.at[kind],
-            dst_ref=far.at[kind],
+            dst_ref=cached.at[kind, pl.ds(tokens, tokens)],
             send_sem=far_send.at[kind],
             recv_sem=far_recv.at[kind],
             device_id=other_group,
@@ -142,83 +160,125 @@
     for copy in far_copies:
         copy.start()
 
+    asked_copy.wait()
+
     def widen(index, carry):
-        at = pl.ds(pl.multiple_of(index * 512, 512), 512)
-        scaled = query_ref[at].astype(HI) * SCALE
+        step, first = index // (samples // 16), 16 * lax.rem(index, samples // 16)
+        base = pl.multiple_of(index * 16 * heads, 16 * heads)
+        for head in range(heads):
+            block = asked[step, pl.ds(pl.multiple_of(first, 16), 16), head * DH : (head + 1) * DH]
+            spread[pl.ds(base + head, 16, stride=heads)] = block.astype(HI)
+        at = pl.ds(base, 16 * heads)
+        plain = spread[at]
+        query_ref[at] = plain.astype(LO)
+        scaled = plain * SCALE
         high = scaled.astype(LO)
         wide[at] = jnp.concatenate([high, (scaled - high.astype(HI)).astype(LO)], axis=1)
         return carry
 
-    lax.fori_loop(0, rows // 512, widen, 0)
+    lax.fori_loop(0, STEPS * samples // 16, widen, 0)
     prompt_copy.wait()
 
-    def prompt_tile(at, source, first):
-        queries = wide[at]
-        top = jnp.full((ROW_TILE, DH), MASKED_SCORE, HI) if first else state_max[at]
-        mixed = None if first else state_out[at]
-        for start in range(0, tokens, TOKEN_BLOCK):
-            span = pl.ds(start, TOKEN_BLOCK)
-            scores = dot_nt(queries, twice(source[0, span]))
-            top, mixed = absorb(scores, source[1, span], top, mixed)
-        return top, mixed
-
-    def tile_rows(index):
-        return pl.ds(pl.multiple_of(index * ROW_TILE, ROW_TILE), ROW_TILE)
-
-    def own_tile(index, carry):
-        at = tile_rows(index)
-        state_max[at], state_out[at] = prompt_tile(at, own, True)
-        return carry
-
-    lax.fori_loop(0, blocks, own_tile, 0)
+    def prompt_rows(begin, count, source):
+        groups = [
+            pl.ds(pl.multiple_of(begin + offset, GROUP_ROWS), GROUP_ROWS)
+            for offset in range(0, count, GROUP_ROWS)
+        ]
+        state = [(state_max[at], state_out[at]) for at in groups]
+        spans = [pl.ds(source * tokens + t, TOKEN_BLOCK) for t in range(0, tokens, TOKEN_BLOCK)]
+        order = [(span, g) for span in spans for g in range(len(groups))]
+
+        def scores_of(span, g):
+            return dot_nt(wide[groups[g]], twice(cached[0, span]))
+
+        following = scores_of(*order[0])
+        for turn_index, (span, g) in enumerate(order):
+            scores = following
+            if turn_index + 1 < len(order):
+                following = scores_of(*order[turn_index + 1])
+            state[g] = absorb(scores, cached[1, span], *state[g])
+        for at, (top, mixed) in zip(groups, state):
+            state_max[at], state_out[at] = top, mixed
+
+    def own_step(index, carry):
+        prompt_rows(index * OWN_ROWS, OWN_ROWS, 0)
+        return carry
+
+    lax.fori_loop(0, rows // OWN_ROWS, own_step, 0)
+
+    def gather_rows(ref, start, count):
+        return jnp.concatenate(
+            [ref[pl.ds(start + s * step_rows, count)] for s in range(STEPS)], axis=0
+        )
+
+    def scatter_rows(ref, start, count, value):
+        for s in range(STEPS):
+            ref[pl.ds(start + s * step_rows, count)] = value[s * count : (s + 1) * count]
 
     for copy in fresh_copies:
         copy.wait()
-    new_rows = 16 * per_sample
-    at = pl.ds(pl.multiple_of(seq * new_rows, new_rows), new_rows)
+    new_rows = 16 * heads
+    start = pl.multiple_of(seq * new_rows, new_rows)
     padding = jnp.zeros((DH - STEPS * 16, DH), LO)
     new_keys = jnp.concatenate([fresh[0, t] for t in range(STEPS)] + [padding], axis=0)
     new_values = jnp.concatenate([fresh[1, t] for t in range(STEPS)] + [padding], axis=0)
-    scores = dot_nt(wide[at], twice(new_keys))
+    scores = dot_nt(gather_rows(query_ref, start, new_rows), new_keys) * SCALE
     row = lax.broadcasted_iota(jnp.int32, scores.shape, 0)
     column = lax.broadcasted_iota(jnp.int32, scores.shape, 1)
-    row_sample = row // per_sample
-    row_step = (row - row_sample * per_sample) // (per_sample // STEPS)
-    seen = (column // 16 <= row_step) & (lax.rem(column, 16) == row_sample)
+    row_sample = lax.rem(row, new_rows) // heads
+    seen = (column // 16 <= row // new_rows) & (lax.rem(column, 16) == row_sample)
     scores = jnp.where(seen, scores, MASKED_SCORE)
-    state_max[at], state_out[at] = absorb(scores, new_values, state_max[at], state_out[at])
-
-    pair_rows = 2 * per_sample
-    row = lax.broadcasted_iota(jnp.int32, (pair_rows, 2 * slots), 0)
-    column = lax.broadcasted_iota(jnp.int32, (pair_rows, 2 * slots), 1)
-    is_first = row < per_sample
+    top, mixed = absorb(
+        scores, new_values, gather_rows(state_max, start, new_rows),
+        gather_rows(state_out, start, new_rows),
+    )
+    scatter_rows(state_max, start, new_rows, top)
+    scatter_rows(state_out, start, new_rows, mixed)
+
+    pair_rows = 2 * heads
+    shape = (STEPS * pair_rows, 2 * slots)
+    column = lax.broadcasted_iota(jnp.int32, shape, 1)
+    is_first = lax.rem(lax.broadcasted_iota(jnp.int32, shape, 0), pair_rows) < heads
     begin = jnp.where(is_first, 0, slots)
 
-    def resident_pair(index):
+    def pair_scores(index):
         first = 2 * index
-        at = pl.ds(pl.multiple_of(index * pair_rows, 32), pair_rows)
-        pair = pl.ds(first, 2)
-        keys = resident[0, pair].reshape(2 * slots, DH)
-        values = resident[1, pair].reshape(2 * slots, DH)
-        scores = dot_nt(wide[at], twice(keys))
+        start = pl.multiple_of(index * pair_rows, pair_rows)
+        keys = resident[0, pl.ds(first, 2)].reshape(2 * slots, DH)
+        scores = dot_nt(gather_rows(query_ref, start, pair_rows), keys) * SCALE
         here = seq * slots
         one = jnp.minimum(lengths_ref[first] - here, slots)
         two = jnp.minimum(lengths_ref[first + 1] - here, slots) + slots
         seen = (column >= begin) & (column < jnp.where(is_first, one, two))
-        scores = jnp.where(seen, scores, MASKED_SCORE)
-        return at, absorb(scores, values, state_max[at], state_out[at])
-
-    def resident_step(index, carry):
-        results = [resident_pair(index * 4 + u) for u in range(4)]
-        for at, (top, mixed) in results:
-            state_max[at] = top
-            state_out[at] = mixed
-        return carry
-
-    steps_per_chunk = chunk // 8
-    for index in range(chunks):
-        resident_copy(index).wait()
-        lax.fori_loop(index * steps_per_chunk, (index + 1) * steps_per_chunk, resident_step, 0)
+        return jnp.where(seen, scores, MASKED_SCORE)
+
+    def pair_weights(index, scores):
+        start = pl.multiple_of(index * pair_rows, pair_rows)
+        old = gather_rows(state_max, start, pair_rows)
+        top = jnp.maximum(old, jnp.max(scores, axis=1, keepdims=True))
+        return top, jnp.exp2(scores - twice(top)).astype(LO), jnp.exp2(old - top)
+
+    def pair_mix(index, weights, decay):
+        start = pl.multiple_of(index * pair_rows, pair_rows)
+        values = resident[1, pl.ds(2 * index, 2)].reshape(2 * slots, DH)
+        mixed = dot_nn(weights, with_ones(values))
+        return gather_rows(state_out, start, pair_rows) * twice(decay) + mixed
+
+    pairs = chunk // 2
+
+    def resident_step(step, carry):
+        resident_copy(step).wait()
+        indices = [step * pairs + u for u in range(pairs)]
+        scores = [pair_scores(index) for index in indices]
+        weighed = [pair_weights(index, s) for index, s in zip(indices, scores)]
+        mixes = [pair_mix(index, w[1], w[2]) for index, w in zip(indices, weighed)]
+        for index, (top, _, _), mixed in zip(indices, weighed, mixes):
+            start = pl.multiple_of(index * pair_rows, pair_rows)
+            scatter_rows(state_max, start, pair_rows, top)
+            scatter_rows(state_out, start, pair_rows, mixed)
+        return carry
+
+    lax.fori_loop(0, chunks, resident_step, 0)
 
     for copy in far_copies:
         copy.wait_recv()
@@ -259,15 +319,16 @@
         )
 
     def far_tile(b):
-        top, mixed = prompt_tile(tile_rows(b), far, False)
+        prompt_rows(b * ROW_TILE, ROW_TILE, 1)
+        top, mixed = state_max[tile_rows(b)], state_out[tile_rows(b)]
         total = mixed[:, DH:]
         mean = (mixed[:, :DH] / total).astype(LO)
         logsum = top + jnp.log(total) * LOG2E
         for index in range(ROW_TILE // PIECE):
             span = slice(index * PIECE, (index + 1) * PIECE)
-            half, owner = index // 4, index % 4
-            part[b, half, owner, 0:PIECE] = mean[span]
-            part[b, half, owner, PIECE:] = encode_logsum(logsum[span])
+            side, owner = index // 4, index % 4
+            part[b, side, owner, 0:PIECE] = mean[span]
+            part[b, side, owner, PIECE:] = encode_logsum(logsum[span])
         swap_copy(b).start()
 
     def join_cores(b):
@@ -294,12 +355,13 @@
 
     def turn(b, carry):
         pl.when(b < blocks)(lambda: far_tile(b))
-        pl.when((b >= 1) & (b < blocks + 1))(lambda: join_cores(b - 1))
-        pl.when((b >= 2) & (b < blocks + 2))(lambda: join_chips(b - 2))
-        pl.when(b >= 3)(lambda: forward(b - 3))
-        return carry
-
-    lax.fori_loop(0, blocks + 3, turn, 0)
+        late, later, last = (b - lag for lag in LAGS)
+        pl.when((late >= 0) & (late < blocks))(lambda: join_cores(late))
+        pl.when((later >= 0) & (later < blocks))(lambda: join_chips(later))
+        pl.when(last >= 0)(lambda: forward(last))
+        return carry
+
+    lax.fori_loop(0, blocks + LAGS[2], turn, 0)
 
     for copy in far_copies:
         copy.wait_send()
@@ -320,8 +382,6 @@
     steps, samples, columns = queries.shape
     heads = columns // DH
     rows = steps * samples * heads
-    query_rows = jnp.transpose(queries.reshape(steps, samples, heads, DH), (1, 0, 2, 3))
-    query_rows = query_rows.reshape(rows, DH)
     blocks = rows // ROW_TILE
     piece = (PIECE + EXTRA, DH)
     dma = pltpu.SemaphoreType.DMA
@@ -330,11 +390,13 @@
     out = pl.pallas_call(
         kernel,
         out_shape=jax.ShapeDtypeStruct((rows, DH), LO),
-        in_specs=[pl.BlockSpec(memory_space=pltpu.SMEM), anywhere, in_vmem, anywhere, anywhere],
+        in_specs=[pl.BlockSpec(memory_space=pltpu.SMEM), anywhere, anywhere, anywhere, anywhere],
         out_specs=in_vmem,
         scratch_shapes=[
-            pltpu.VMEM(prompt_kv.shape, LO),
-            pltpu.VMEM(prompt_kv.shape, LO),
+            pltpu.VMEM((2, 2 * prompt_kv.shape[1], DH), LO),
+            pltpu.VMEM(queries.shape, LO),
+            pltpu.VMEM((rows, DH), HI),
+            pltpu.VMEM((rows, DH), LO),
             pltpu.VMEM((rows, 2 * DH), LO),
             pltpu.VMEM(resident_kv.shape, LO),
             pltpu.VMEM((2, steps, 16, DH), LO),
@@ -344,15 +406,14 @@
             pltpu.VMEM((blocks, 4) + piece, LO),
             pltpu.VMEM((blocks, 4) + piece, LO),
             pltpu.VMEM((blocks, 3) + piece, LO),
-            dma((3,)), dma((4,)), dma((2,)), dma((2,)), dma((blocks,)), dma((blocks,)),
+            dma((4,)), dma((4,)), dma((2,)), dma((2,)), dma((blocks,)), dma((blocks,)),
             dma((blocks, 3)), dma((blocks, 3)), dma((blocks, 3)), dma((blocks, 3)),
             dma((blocks,)), dma((blocks,)),
         ],
         compiler_params=pltpu.CompilerParams(
-            collective_id=0, has_side_effects=True, vmem_limit_bytes=58 * 2**20
+            collective_id=0, has_side_effects=True, vmem_limit_bytes=48 * 2**20
         ),
-    )(seq_lengths, prompt_kv, query_rows, new_kv, resident_kv)
-    out = jnp.transpose(out.reshape(samples, steps, heads, DH), (1, 0, 2, 3))
+    )(seq_lengths, prompt_kv, queries, new_kv, resident_kv)
     return out.reshape(queries.shape)
 
 

time: 87.6 us -> 70.4 us (0.80)
  Pallas kernels: 80.5 us -> 63.9 us
    pallas_call x1, Pallas kernels: 80.5 us -> 63.9 us  [local(): pl.pallas_call(kernel, out_shape=jax.ShapeDtypeStruct((rows, DH), LO), in...]
    unnamed x1 -> x8, local copies, waits for them, and re-layouts: 1.81 us -> 4.21 us
    transpose x1 -> x0, local copies, waits for them, and re-layouts: 1.68 us -> none  [local(): out = jnp.transpose(out.reshape(samples, steps, heads, DH), (1, 0, 2, 3))]
    reshape x1 -> x0, local copies, waits for them, and re-layouts: 1.42 us -> none  [local(): queries.reshape(steps, samples, heads, DH)]
where the time goes in v2:
time: 70.4 us; the launch traced here: 70.2 us
  Pallas kernels  63.9 us (91%)
  local copies, waits for them, and re-layouts  6.27 us (9%)
    pallas_call x1, Pallas kernels, local(): pl.pallas_call(kernel, out_shape=jax.ShapeDtypeStruct((rows, DH), LO), in...  63.9 us
    unnamed x8, local copies, waits for them, and re-layouts  4.21 us
    reshape x1, local copies, waits for them, and re-layouts, local(): return out.reshape(queries.shape)  2.06 us

profile of v2, /device:TPU:1, one launch (start us, length us, event | category | flops | bytes accessed | tf_op | source)
XLA Modules:
  0.0 70.2 jit_solution(15461564633740635250)
XLA Ops:
  0.0 0.0 copy-start
  0.0 1.4 %copy-done = bf16[3,128,2048]{2,1,0:T(8,128)(2,1)S(1)} copy-done((bf16[3,128,2048]{2,1,0:T(8,128)(2,1)S(1)}, bf16[3,128,2048]{2,1,0:T(8,128)(2,1)}, u32[]{:S(2)}) %copy-start) | copy-done | bytes 1572888
  1.4 0.0 copy-start.1
  1.4 1.2 %copy-done.1 = bf16[2,2048,128]{2,1,0:T(8,128)(2,1)S(1)} copy-done((bf16[2,2048,128]{2,1,0:T(8,128)(2,1)S(1)}, bf16[2,2048,128]{2,1,0:T(8,128)(2,1)}, u32[]{:S(2)}) %copy-start.1) | copy-done | bytes 1048600
  2.6 0.0 copy-start.2
  2.6 0.9 %copy-done.2 = bf16[2,3,128,128]{3,2,1,0:T(8,128)(2,1)S(1)} copy-done((bf16[2,3,128,128]{3,2,1,0:T(8,128)(2,1)S(1)}, bf16[2,3,128,128]{3,2,1,0:T(8,128)(2,1)}, u32[]{:S(2)}) %copy-start.2) | copy-done | bytes 196632
  3.6 0.0 copy-start.3
  3.6 0.7 copy-done.3
  4.2 63.9 %shard_map.55 = bf16[6144,128]{1,0:T(8,128)(2,1)S(1)} custom-call(s32[128]{0:T(128)S(1)} %copy-done.3, bf16[2,2048,128]{2,1,0:T(8,128)(2,1)S(1)} %copy-done.1, bf16[3,128,2048]{2,1,0:T(8,128)(2,1)S(1)} %copy-done, bf16[2,3,128,128]{3,2,1,0:T(8,128)(2,1)S(1)} %copy-done.2, bf16[2,128,128,128]{3,2,1,0:T(8,128)(2,1)} %resident_ref.1), custom_call_target="tpu_custom_call" | custom-call | tf_op jit(solution)/shard_map/pallas_call | solution.py:390
  68.1 2.1 %reshape.3 = bf16[3,128,2048]{2,1,0:T(8,128)(2,1)} reshape(bf16[6144,128]{1,0:T(8,128)(2,1)S(1)} %shard_map.55) | data formatting | bytes 3145728 | tf_op jit(solution)/shard_map/reshape | solution.py:417
Async XLA Ops:
  0.0 1.4 %copy-start = (bf16[3,128,2048]{2,1,0:T(8,128)(2,1)S(1)}, bf16[3,128,2048]{2,1,0:T(8,128)(2,1)}, u32[]{:S(2)}) copy-start(bf16[3,128,2048]{2,1,0:T(8,128)(2,1)} %asked_ref.1) | copy-start | bytes 4718596
  1.4 1.2 %copy-start.1 = (bf16[2,2048,128]{2,1,0:T(8,128)(2,1)S(1)}, bf16[2,2048,128]{2,1,0:T(8,128)(2,1)}, u32[]{:S(2)}) copy-start(bf16[2,2048,128]{2,1,0:T(8,128)(2,1)} %prompt_ref.1) | copy-start | bytes 3145732
  2.6 0.9 %copy-start.2 = (bf16[2,3,128,128]{3,2,1,0:T(8,128)(2,1)S(1)}, bf16[2,3,128,128]{3,2,1,0:T(8,128)(2,1)}, u32[]{:S(2)}) copy-start(bf16[2,3,128,128]{3,2,1,0:T(8,128)(2,1)} %new_ref.1) | copy-start | bytes 589828
  3.6 0.7 copy-start.3

commit v3 on v2

--- a/solution.py
+++ b/solution.py
@@ -12,11 +12,12 @@
 SCALE = LOG2E * DH**-0.5
 MESH = pl.DeviceIdType.MESH
 
-ROW_TILE = 1024
-OWN_ROWS = 2048
+ROW_TILE = 512
+OWN_ROWS = 1536
 GROUP_ROWS = 256
 TOKEN_BLOCK = 1024
-LAGS = (1, 3, 5)
+EARLY = 2
+LAGS = (2, 3)
 PIECE = 128
 EXTRA = 16
 HI, LO = jnp.float32, jnp.bfloat16
@@ -48,8 +49,14 @@
     return new_max, mixed
 
 
+def on_diagonal():
+    row = lax.broadcasted_iota(jnp.int32, (PIECE, DH), 0)
+    return row == lax.broadcasted_iota(jnp.int32, (PIECE, DH), 1)
+
+
 def encode_logsum(logsum):
-    flat = jnp.transpose(logsum)[0:EXTRA]
+    flat = jnp.sum(jnp.where(on_diagonal(), logsum, 0.0), axis=0, keepdims=True)
+    flat = jnp.broadcast_to(flat, (EXTRA, DH))
     high = flat.astype(LO).astype(HI)
     middle = (flat - high).astype(LO).astype(HI)
     low = flat - high - middle
@@ -62,7 +69,8 @@
 def decode_logsum(coded):
     parts = coded.astype(HI)
     flat = parts[0:1] + parts[1:2] + parts[2:3]
-    return jnp.transpose(jnp.broadcast_to(flat, (PIECE, DH)))
+    own = jnp.where(on_diagonal(), jnp.broadcast_to(flat, (PIECE, DH)), 0.0)
+    return jnp.broadcast_to(jnp.sum(own, axis=1, keepdims=True), (PIECE, DH))
 
 
 def merge(pieces):
@@ -83,12 +91,15 @@
     lengths_ref, prompt_ref, asked_ref, new_ref, resident_ref, out_ref,
     cached, asked, spread, query_ref, wide, resident, fresh, state_max, state_out,
     part, swapped, joined, crossed,
-    local_sems, resident_sems, far_send, far_recv, swap_send, swap_recv,
+    local_sems, resident_sems, near_send, near_recv, far_send, far_recv,
+    relay_send, relay_recv, swap_send, swap_recv,
     cross_send, cross_recv, gather_send, gather_recv, forward_send, forward_recv,
+    last_send, last_recv,
 ):
     samples = lengths_ref.shape[0]
     rows = query_ref.shape[0]
-    blocks = rows // ROW_TILE
+    core_rows = rows // 2
+    blocks = core_rows // ROW_TILE
     step_rows = rows // STEPS
     heads = step_rows // samples
     slots = resident_ref.shape[2]
@@ -96,13 +107,16 @@
     group = lax.axis_index("group")
     seq = lax.axis_index("seq")
     x, core = seq // 2, lax.rem(seq, 2)
+    core_start = core * core_rows
     other_group = {"group": 1 - group}
     other_core = {"seq": 2 * x + 1 - core}
     peers = [lax.rem(x + d, 4) for d in (1, 2, 3)]
     sources = [lax.rem(x + 4 - d, 4) for d in (1, 2, 3)]
 
     barrier = pltpu.get_barrier_semaphore()
-    greeted = [other_group, other_core] + [{"seq": 2 * p + core} for p in peers]
+    greeted = [other_group, other_core] + [
+        {"seq": 2 * p + side} for p in peers for side in (0, 1)
+    ]
     for device in greeted:
         pl.semaphore_signal(barrier, inc=1, device_id=device, device_id_type=MESH)
 
@@ -135,29 +149,34 @@
     for index in range(chunks):
         resident_copy(index).start()
 
-    def tile_rows(index):
-        return pl.ds(pl.multiple_of(index * ROW_TILE, ROW_TILE), ROW_TILE)
-
     def clear(index, carry):
-        state_max[tile_rows(index)] = jnp.full((ROW_TILE, DH), MASKED_SCORE, HI)
-        state_out[tile_rows(index)] = jnp.zeros((ROW_TILE, 2 * DH), HI)
-        return carry
-
-    lax.fori_loop(0, blocks, clear, 0)
+        at = pl.ds(pl.multiple_of(index * 512, 512), 512)
+        state_max[at] = jnp.full((512, DH), MASKED_SCORE, HI)
+        state_out[at] = jnp.zeros((512, 2 * DH), HI)
+        return carry
+
+    lax.fori_loop(0, rows // 512, clear, 0)
 
     pl.semaphore_wait(barrier, len(greeted))
-    far_copies = [
-        pltpu.make_async_remote_copy(
-            src_ref=prompt_ref.at[kind],
-            dst_ref=cached.at[kind, pl.ds(tokens, tokens)],
-            send_sem=far_send.at[kind],
-            recv_sem=far_recv.at[kind],
-            device_id=other_group,
-            device_id_type=MESH,
-        )
-        for kind in (0, 1)
-    ]
-    for copy in far_copies:
+    def token_copies(source, source_start, start, send, recv, device):
+        return [
+            pltpu.make_async_remote_copy(
+                src_ref=source.at[kind, pl.ds(source_start, tokens)],
+                dst_ref=cached.at[kind, pl.ds(start, tokens)],
+                send_sem=send.at[kind],
+                recv_sem=recv.at[kind],
+                device_id=device,
+                device_id_type=MESH,
+            )
+            for kind in (0, 1)
+        ]
+
+    far_copies = token_copies(prompt_ref, 0, 2 * tokens, far_send, far_recv, other_group)
+    near_copies = token_copies(prompt_ref, 0, tokens, near_send, near_recv, other_core)
+    relay_copies = token_copies(
+        cached, 2 * tokens, 3 * tokens, relay_send, relay_recv, other_core
+    )
+    for copy in far_copies + near_copies:
         copy.start()
 
     asked_copy.wait()
@@ -177,34 +196,6 @@
         return carry
 
     lax.fori_loop(0, STEPS * samples // 16, widen, 0)
-    prompt_copy.wait()
-
-    def prompt_rows(begin, count, source):
-        groups = [
-            pl.ds(pl.multiple_of(begin + offset, GROUP_ROWS), GROUP_ROWS)
-            for offset in range(0, count, GROUP_ROWS)
-        ]
-        state = [(state_max[at], state_out[at]) for at in groups]
-        spans = [pl.ds(source * tokens + t, TOKEN_BLOCK) for t in range(0, tokens, TOKEN_BLOCK)]
-        order = [(span, g) for span in spans for g in range(len(groups))]
-
-        def scores_of(span, g):
-            return dot_nt(wide[groups[g]], twice(cached[0, span]))
-
-        following = scores_of(*order[0])
-        for turn_index, (span, g) in enumerate(order):
-            scores = following
-            if turn_index + 1 < len(order):
-                following = scores_of(*order[turn_index + 1])
-            state[g] = absorb(scores, cached[1, span], *state[g])
-        for at, (top, mixed) in zip(groups, state):
-            state_max[at], state_out[at] = top, mixed
-
-    def own_step(index, carry):
-        prompt_rows(index * OWN_ROWS, OWN_ROWS, 0)
-        return carry
-
-    lax.fori_loop(0, rows // OWN_ROWS, own_step, 0)
 
     def gather_rows(ref, start, count):
         return jnp.concatenate(
@@ -280,15 +271,66 @@
 
     lax.fori_loop(0, chunks, resident_step, 0)
 
-    for copy in far_copies:
+    def piece_state(at):
+        total = state_out[at, DH:]
+        return state_out[at, :DH] / total, state_max[at] + jnp.log(total) * LOG2E
+
+    def pack_step(index, carry):
+        for u in range(4):
+            start = (core_rows - core_start) + (4 * index + u) * PIECE
+            mean, logsum = piece_state(pl.ds(pl.multiple_of(start, PIECE), PIECE))
+            part[4 * index + u, 0:PIECE] = mean.astype(LO)
+            part[4 * index + u, PIECE:] = encode_logsum(logsum)
+        return carry
+
+    lax.fori_loop(0, blocks, pack_step, 0)
+    swap_copy = pltpu.make_async_remote_copy(
+        src_ref=part, dst_ref=swapped, send_sem=swap_send, recv_sem=swap_recv,
+        device_id=other_core, device_id_type=MESH,
+    )
+    swap_copy.start()
+
+    def prompt_rows(begin, count, first, length):
+        groups = [
+            pl.ds(pl.multiple_of(begin + offset, GROUP_ROWS), GROUP_ROWS)
+            for offset in range(0, count, GROUP_ROWS)
+        ]
+        state = [(state_max[at], state_out[at]) for at in groups]
+        spans = [pl.ds(t, TOKEN_BLOCK) for t in range(first, first + length, TOKEN_BLOCK)]
+        order = [(span, g) for span in spans for g in range(len(groups))]
+
+        def scores_of(span, g):
+            return dot_nt(wide[groups[g]], twice(cached[0, span]))
+
+        following = scores_of(*order[0])
+        for turn_index, (span, g) in enumerate(order):
+            scores = following
+            if turn_index + 1 < len(order):
+                following = scores_of(*order[turn_index + 1])
+            state[g] = absorb(scores, cached[1, span], *state[g])
+        for at, (top, mixed) in zip(groups, state):
+            state_max[at], state_out[at] = top, mixed
+
+    def own_step(index, carry):
+        prompt_rows(core_start + index * OWN_ROWS, OWN_ROWS, 0, 2 * tokens)
+        return carry
+
+    prompt_copy.wait()
+    for copy in near_copies:
         copy.wait_recv()
-
-    def swap_copy(b):
-        return pltpu.make_async_remote_copy(
-            src_ref=part.at[b, 1 - core], dst_ref=swapped.at[b],
-            send_sem=swap_send.at[b], recv_sem=swap_recv.at[b],
-            device_id=other_core, device_id_type=MESH,
-        )
+    lax.fori_loop(0, core_rows // OWN_ROWS, own_step, 0)
+    swap_copy.wait_recv()
+    for far_copy, relay_copy in zip(far_copies, relay_copies):
+        far_copy.wait_recv()
+        relay_copy.start()
+
+    def early_step(b, carry):
+        prompt_rows(core_start + b * ROW_TILE, ROW_TILE, 2 * tokens, tokens)
+        return carry
+
+    lax.fori_loop(0, EARLY, early_step, 0)
+    for relay_copy in relay_copies:
+        relay_copy.wait_recv()
 
     def cross_copy(b, d):
         return pltpu.make_async_remote_copy(
@@ -298,7 +340,7 @@
         )
 
     def piece_rows(b, owner):
-        start = b * ROW_TILE + core * (ROW_TILE // 2) + owner * PIECE
+        start = core_start + b * ROW_TILE + owner * PIECE
         return pl.ds(pl.multiple_of(start, PIECE), PIECE)
 
     def gather_copy(b, d, owner):
@@ -309,9 +351,18 @@
             device_id={"seq": 2 * peers[d] + core}, device_id_type=MESH,
         )
 
-    def forward_copy(b, half):
-        start = b * ROW_TILE + half * (ROW_TILE // 2)
-        at = pl.ds(pl.multiple_of(start, ROW_TILE // 2), ROW_TILE // 2)
+    def last_copy(d, owner):
+        at = piece_rows(blocks - 1, owner)
+        target = 2 * (x if d == 3 else peers[d]) + 1 - core
+        return pltpu.make_async_remote_copy(
+            src_ref=out_ref.at[at], dst_ref=out_ref.at[at],
+            send_sem=last_send.at[d], recv_sem=last_recv.at[d],
+            device_id={"seq": target}, device_id_type=MESH,
+        )
+
+    def forward_copy(b, side):
+        start = side * core_rows + b * ROW_TILE
+        at = pl.ds(pl.multiple_of(start, ROW_TILE), ROW_TILE)
         return pltpu.make_async_remote_copy(
             src_ref=out_ref.at[at], dst_ref=out_ref.at[at],
             send_sem=forward_send.at[b], recv_sem=forward_recv.at[b],
@@ -319,24 +370,26 @@
         )
 
     def far_tile(b):
-        prompt_rows(b * ROW_TILE, ROW_TILE, 1)
-        top, mixed = state_max[tile_rows(b)], state_out[tile_rows(b)]
-        total = mixed[:, DH:]
-        mean = (mixed[:, :DH] / total).astype(LO)
-        logsum = top + jnp.log(total) * LOG2E
-        for index in range(ROW_TILE // PIECE):
-            span = slice(index * PIECE, (index + 1) * PIECE)
-            side, owner = index // 4, index % 4
-            part[b, side, owner, 0:PIECE] = mean[span]
-            part[b, side, owner, PIECE:] = encode_logsum(logsum[span])
-        swap_copy(b).start()
-
-    def join_cores(b):
-        swap_copy(b).wait_recv()
+        begin = core_start + b * ROW_TILE
+
+        @pl.when(b < EARLY)
+        def _():
+            prompt_rows(begin, ROW_TILE, 3 * tokens, tokens)
+
+        @pl.when(b >= EARLY)
+        def _():
+            prompt_rows(begin, ROW_TILE, 2 * tokens, 2 * tokens)
+
         for owner in range(4):
-            mean, logsum = merge([part[b, core, owner], swapped[b, owner]])
-            joined[b, owner, 0:PIECE] = mean.astype(LO)
-            joined[b, owner, PIECE:] = encode_logsum(logsum)
+            at = piece_rows(b, owner)
+            other = swapped[4 * b + owner]
+            other_logsum = decode_logsum(other[PIECE:])
+            top = jnp.maximum(state_max[at], other_logsum)
+            decay, share = jnp.exp2(state_max[at] - top), jnp.exp2(other_logsum - top)
+            total = state_out[at, DH:] * decay + share
+            mixed = state_out[at, :DH] * decay + other[:PIECE].astype(HI) * share
+            joined[b, owner, 0:PIECE] = (mixed / total).astype(LO)
+            joined[b, owner, PIECE:] = encode_logsum(top + jnp.log(total) * LOG2E)
         for d in range(3):
             cross_copy(b, d).start()
 
@@ -348,41 +401,59 @@
         for d in range(3):
             gather_copy(b, d, x).start()
 
+        @pl.when(b == blocks - 1)
+        def _():
+            for d in range(4):
+                last_copy(d, x).start()
+
     def forward(b):
         for d in range(3):
             gather_copy(b, d, sources[d]).wait_recv()
-        forward_copy(b, core).start()
+        pl.when(b < blocks - 1)(lambda: forward_copy(b, core).start())
 
     def turn(b, carry):
         pl.when(b < blocks)(lambda: far_tile(b))
-        late, later, last = (b - lag for lag in LAGS)
-        pl.when((late >= 0) & (late < blocks))(lambda: join_cores(late))
-        pl.when((later >= 0) & (later < blocks))(lambda: join_chips(later))
+        late, last = (b - lag for lag in LAGS)
+        pl.when((late >= 0) & (late < blocks))(lambda: join_chips(late))
         pl.when(last >= 0)(lambda: forward(last))
         return carry
 
-    lax.fori_loop(0, blocks + LAGS[2], turn, 0)
-
-    for copy in far_copies:
+    lax.fori_loop(0, blocks + LAGS[1], turn, 0)
+
+    for copy in far_copies + near_copies + relay_copies + [swap_copy]:
         copy.wait_send()
 
     def finish(b, carry):
-        swap_copy(b).wait_send()
         for d in range(3):
             cross_copy(b, d).wait_send()
             gather_copy(b, d, x).wait_send()
-        forward_copy(b, core).wait_send()
-        forward_copy(b, 1 - core).wait_recv()
+
+        @pl.when(b < blocks - 1)
+        def _():
+            forward_copy(b, core).wait_send()
+            forward_copy(b, 1 - core).wait_recv()
+
         return carry
 
     lax.fori_loop(0, blocks, finish, 0)
+    for d in range(4):
+        last_copy(d, x).wait_send()
+        at = pl.ds(
+            pl.multiple_of(core_rows - core_start + (blocks - 1) * ROW_TILE, PIECE), ROW_TILE
+        )
+        owner = x if d == 3 else sources[d]
+        piece = out_ref.at[at].at[pl.ds(pl.multiple_of(owner * PIECE, PIECE), PIECE)]
+        pltpu.make_async_remote_copy(
+            src_ref=piece, dst_ref=piece, send_sem=last_send.at[d], recv_sem=last_recv.at[d],
+            device_id=other_core, device_id_type=MESH,
+        ).wait_recv()
 
 
 def local(prompt_kv, queries, new_kv, resident_kv, seq_lengths):
     steps, samples, columns = queries.shape
     heads = columns // DH
     rows = steps * samples * heads
-    blocks = rows // ROW_TILE
+    blocks = rows // 2 // ROW_TILE
     piece = (PIECE + EXTRA, DH)
     dma = pltpu.SemaphoreType.DMA
     anywhere = pl.BlockSpec(memory_space=pl.ANY)
@@ -393,7 +464,7 @@
         in_specs=[pl.BlockSpec(memory_space=pltpu.SMEM), anywhere, anywhere, anywhere, anywhere],
         out_specs=in_vmem,
         scratch_shapes=[
-            pltpu.VMEM((2, 2 * prompt_kv.shape[1], DH), LO),
+            pltpu.VMEM((2, 4 * prompt_kv.shape[1], DH), LO),
             pltpu.VMEM(queries.shape, LO),
             pltpu.VMEM((rows, DH), HI),
             pltpu.VMEM((rows, DH), LO),
@@ -402,13 +473,14 @@
             pltpu.VMEM((2, steps, 16, DH), LO),
             pltpu.VMEM((rows, DH), HI),
             pltpu.VMEM((rows, 2 * DH), HI),
-            pltpu.VMEM((blocks, 2, 4) + piece, LO),
-            pltpu.VMEM((blocks, 4) + piece, LO),
+            pltpu.VMEM((4 * blocks,) + piece, LO),
+            pltpu.VMEM((4 * blocks,) + piece, LO),
             pltpu.VMEM((blocks, 4) + piece, LO),
             pltpu.VMEM((blocks, 3) + piece, LO),
-            dma((4,)), dma((4,)), dma((2,)), dma((2,)), dma((blocks,)), dma((blocks,)),
+            dma((4,)), dma((4,)), dma((2,)), dma((2,)), dma((2,)), dma((2,)),
+            dma((2,)), dma((2,)), dma, dma,
             dma((blocks, 3)), dma((blocks, 3)), dma((blocks, 3)), dma((blocks, 3)),
-            dma((blocks,)), dma((blocks,)),
+            dma((blocks,)), dma((blocks,)), dma((4,)), dma((4,)),
         ],
         compiler_params=pltpu.CompilerParams(
             collective_id=0, has_side_effects=True, vmem_limit_bytes=48 * 2**20

time: 70.4 us -> 69.8 us (level)
  no operation moved by 1% of the time
where the time goes in v3:
time: 69.8 us; the launch traced here: 69.6 us
  Pallas kernels  63.3 us (91%)
  local copies, waits for them, and re-layouts  6.27 us (9%)
    pallas_call x1, Pallas kernels, local(): pl.pallas_call(kernel, out_shape=jax.ShapeDtypeStruct((rows, DH), LO), in...  63.3 us
    unnamed x8, local copies, waits for them, and re-layouts  4.21 us
    reshape x1, local copies, waits for them, and re-layouts, local(): return out.reshape(queries.shape)  2.06 us

profile of v3, /device:TPU:1, one launch (start us, length us, event | category | flops | bytes accessed | tf_op | source)
XLA Modules:
  0.0 69.6 jit_solution(15194641192273581472)
XLA Ops:
  0.0 0.0 copy-start
  0.0 1.4 %copy-done = bf16[3,128,2048]{2,1,0:T(8,128)(2,1)S(1)} copy-done((bf16[3,128,2048]{2,1,0:T(8,128)(2,1)S(1)}, bf16[3,128,2048]{2,1,0:T(8,128)(2,1)}, u32[]{:S(2)}) %copy-start) | copy-done | bytes 1572888
  1.4 0.0 copy-start.1
  1.4 1.2 %copy-done.1 = bf16[2,2048,128]{2,1,0:T(8,128)(2,1)S(1)} copy-done((bf16[2,2048,128]{2,1,0:T(8,128)(2,1)S(1)}, bf16[2,2048,128]{2,1,0:T(8,128)(2,1)}, u32[]{:S(2)}) %copy-start.1) | copy-done | bytes 1048600
  2.6 0.0 copy-start.2
  2.6 0.9 %copy-done.2 = bf16[2,3,128,128]{3,2,1,0:T(8,128)(2,1)S(1)} copy-done((bf16[2,3,128,128]{3,2,1,0:T(8,128)(2,1)S(1)}, bf16[2,3,128,128]{3,2,1,0:T(8,128)(2,1)}, u32[]{:S(2)}) %copy-start.2) | copy-done | bytes 196632
  3.6 0.0 copy-start.3
  3.6 0.7 copy-done.3
  4.2 63.3 %shard_map.55 = bf16[6144,128]{1,0:T(8,128)(2,1)S(1)} custom-call(s32[128]{0:T(128)S(1)} %copy-done.3, bf16[2,2048,128]{2,1,0:T(8,128)(2,1)S(1)} %copy-done.1, bf16[3,128,2048]{2,1,0:T(8,128)(2,1)S(1)} %copy-done, bf16[2,3,128,128]{3,2,1,0:T(8,128)(2,1)S(1)} %copy-done.2, bf16[2,128,128,128]{3,2,1,0:T(8,128)(2,1)} %resident_ref.1), custom_call_target="tpu_custom_call" | custom-call | tf_op jit(solution)/shard_map/pallas_call | solution.py:461
  67.5 2.1 %reshape.3 = bf16[3,128,2048]{2,1,0:T(8,128)(2,1)} reshape(bf16[6144,128]{1,0:T(8,128)(2,1)S(1)} %shard_map.55) | data formatting | bytes 3145728 | tf_op jit(solution)/shard_map/reshape | solution.py:489
Async XLA Ops:
  0.0 1.4 %copy-start = (bf16[3,128,2048]{2,1,0:T(8,128)(2,1)S(1)}, bf16[3,128,2048]{2,1,0:T(8,128)(2,1)}, u32[]{:S(2)}) copy-start(bf16[3,128,2048]{2,1,0:T(8,128)(2,1)} %asked_ref.1) | copy-start | bytes 4718596
  1.4 1.2 %copy-start.1 = (bf16[2,2048,128]{2,1,0:T(8,128)(2,1)S(1)}, bf16[2,2048,128]{2,1,0:T(8,128)(2,1)}, u32[]{:S(2)}) copy-start(bf16[2,2048,128]{2,1,0:T(8,128)(2,1)} %prompt_ref.1) | copy-start | bytes 3145732
  2.6 0.9 %copy-start.2 = (bf16[2,3,128,128]{3,2,1,0:T(8,128)(2,1)S(1)}, bf16[2,3,128,128]{3,2,1,0:T(8,128)(2,1)}, u32[]{:S(2)}) copy-start(bf16[2,3,128,128]{3,2,1,0:T(8,128)(2,1)} %new_ref.1) | copy-start | bytes 589828
  3.6 0.7 copy-start.3

commit v4 on v3

--- a/solution.py
+++ b/solution.py
@@ -16,6 +16,7 @@
 OWN_ROWS = 1536
 GROUP_ROWS = 256
 TOKEN_BLOCK = 1024
+FARTHEST_FIRST = (1, 0, 2)
 EARLY = 2
 LAGS = (2, 3)
 PIECE = 128
@@ -390,7 +391,7 @@
             mixed = state_out[at, :DH] * decay + other[:PIECE].astype(HI) * share
             joined[b, owner, 0:PIECE] = (mixed / total).astype(LO)
             joined[b, owner, PIECE:] = encode_logsum(top + jnp.log(total) * LOG2E)
-        for d in range(3):
+        for d in FARTHEST_FIRST:
             cross_copy(b, d).start()
 
     def join_chips(b):
@@ -398,7 +399,7 @@
             cross_copy(b, d).wait_recv()
         mean, _ = merge([joined[b, x]] + [crossed[b, d] for d in range(3)])
         out_ref[piece_rows(b, x)] = mean.astype(LO)
-        for d in range(3):
+        for d in FARTHEST_FIRST:
             gather_copy(b, d, x).start()
 
         @pl.when(b == blocks - 1)

time: 69.8 us -> 69.1 us (0.990)
  Pallas kernels: 63.3 us -> 62.6 us
    pallas_call x1, Pallas kernels: 63.3 us -> 62.6 us  [local(): pl.pallas_call(kernel, out_shape=jax.ShapeDtypeStruct((rows, DH), LO), in...]
where the time goes in v4:
time: 69.1 us; the launch traced here: 68.8 us
  Pallas kernels  62.6 us (91%)
  local copies, waits for them, and re-layouts  6.27 us (9%)
    pallas_call x1, Pallas kernels, local(): pl.pallas_call(kernel, out_shape=jax.ShapeDtypeStruct((rows, DH), LO), in...  62.6 us
    unnamed x8, local copies, waits for them, and re-layouts  4.21 us
    reshape x1, local copies, waits for them, and re-layouts, local(): return out.reshape(queries.shape)  2.06 us

profile of v4, /device:TPU:1, one launch (start us, length us, event | category | flops | bytes accessed | tf_op | source)
XLA Modules:
  0.0 68.8 jit_solution(5177523245237809759)
XLA Ops:
  0.0 0.0 copy-start
  0.0 1.4 %copy-done = bf16[3,128,2048]{2,1,0:T(8,128)(2,1)S(1)} copy-done((bf16[3,128,2048]{2,1,0:T(8,128)(2,1)S(1)}, bf16[3,128,2048]{2,1,0:T(8,128)(2,1)}, u32[]{:S(2)}) %copy-start) | copy-done | bytes 1572888
  1.4 0.0 copy-start.1
  1.4 1.2 %copy-done.1 = bf16[2,2048,128]{2,1,0:T(8,128)(2,1)S(1)} copy-done((bf16[2,2048,128]{2,1,0:T(8,128)(2,1)S(1)}, bf16[2,2048,128]{2,1,0:T(8,128)(2,1)}, u32[]{:S(2)}) %copy-start.1) | copy-done | bytes 1048600
  2.6 0.0 copy-start.2
  2.6 0.9 %copy-done.2 = bf16[2,3,128,128]{3,2,1,0:T(8,128)(2,1)S(1)} copy-done((bf16[2,3,128,128]{3,2,1,0:T(8,128)(2,1)S(1)}, bf16[2,3,128,128]{3,2,1,0:T(8,128)(2,1)}, u32[]{:S(2)}) %copy-start.2) | copy-done | bytes 196632
  3.6 0.0 copy-start.3
  3.6 0.7 copy-done.3
  4.2 62.6 %shard_map.55 = bf16[6144,128]{1,0:T(8,128)(2,1)S(1)} custom-call(s32[128]{0:T(128)S(1)} %copy-done.3, bf16[2,2048,128]{2,1,0:T(8,128)(2,1)S(1)} %copy-done.1, bf16[3,128,2048]{2,1,0:T(8,128)(2,1)S(1)} %copy-done, bf16[2,3,128,128]{3,2,1,0:T(8,128)(2,1)S(1)} %copy-done.2, bf16[2,128,128,128]{3,2,1,0:T(8,128)(2,1)} %resident_ref.1), custom_call_target="tpu_custom_call" | custom-call | tf_op jit(solution)/shard_map/pallas_call | solution.py:462
  66.8 2.1 %reshape.3 = bf16[3,128,2048]{2,1,0:T(8,128)(2,1)} reshape(bf16[6144,128]{1,0:T(8,128)(2,1)S(1)} %shard_map.55) | data formatting | bytes 3145728 | tf_op jit(solution)/shard_map/reshape | solution.py:490
Async XLA Ops:
  0.0 1.4 %copy-start = (bf16[3,128,2048]{2,1,0:T(8,128)(2,1)S(1)}, bf16[3,128,2048]{2,1,0:T(8,128)(2,1)}, u32[]{:S(2)}) copy-start(bf16[3,128,2048]{2,1,0:T(8,128)(2,1)} %asked_ref.1) | copy-start | bytes 4718596
  1.4 1.2 %copy-start.1 = (bf16[2,2048,128]{2,1,0:T(8,128)(2,1)S(1)}, bf16[2,2048,128]{2,1,0:T(8,128)(2,1)}, u32[]{:S(2)}) copy-start(bf16[2,2048,128]{2,1,0:T(8,128)(2,1)} %prompt_ref.1) | copy-start | bytes 3145732
  2.6 0.9 %copy-start.2 = (bf16[2,3,128,128]{3,2,1,0:T(8,128)(2,1)S(1)}, bf16[2,3,128,128]{3,2,1,0:T(8,128)(2,1)}, u32[]{:S(2)}) copy-start(bf16[2,3,128,128]{3,2,1,0:T(8,128)(2,1)} %new_ref.1) | copy-start | bytes 589828
  3.6 0.7 copy-start.3
